TPU v7x, 32 devices: a whole 2x2x4 slice. The times are simulated.
32 devices in a mesh: groups: 2 (over y), seq: 4 (over z), dp: 4 (over x, core).
Axes of the slice: x: 2, y: 2, z: 4, core: 2. Of those that a mesh axis runs over, the one named last changes fastest.
Arguments:
- x_raw: bfloat16 [1024, 8192], P(('groups', 'seq'), 'dp'), parts along dimension 0, may hold values from -6 to 6
- bc_raw: bfloat16 [1024, 2048], P(('groups', 'seq'), 'dp'), parts along dimension 0, may hold values from -6 to 6
- z_gate: bfloat16 [1024, 8192], P(('groups', 'seq'), 'dp'), parts along dimension 0, may hold values from -6 to 6
- dt_raw: float32 [1024, 128], P(('groups', 'seq'), 'dp'), parts along dimension 0, may hold values from -3 to 6
- conv_x_weight: float32 [4, 8192], P(None, 'dp'), may hold values from -3 to 3
- conv_x_bias: float32 [8192], P('dp'), may hold values from -3 to 3
- conv_bc_weight: float32 [4, 2048], P(None, 'dp'), may hold values from -3 to 3
- conv_bc_bias: float32 [2048], P('dp'), may hold values from -3 to 3
- dt_bias: float32 [128], P('dp'), may hold values from -1 to 1
- a_log: float32 [128], P('dp')
- skip_d: float32 [128], P('dp'), may hold values from 0.5 to 1.5
- norm_gain: float32 [8192], P('dp'), may hold values from 0.5 to 1.5
- queries: bfloat16 [1024, 4096], P(('groups', 'seq'), 'dp'), parts along dimension 0, may hold values from -6 to 6
- keys: bfloat16 [1024, 1024], P(('groups', 'seq'), 'dp'), parts along dimension 0, may hold values from -6 to 6
- values: bfloat16 [1024, 1024], P(('groups', 'seq'), 'dp'), parts along dimension 0, may hold values from -6 to 6
- doc_lens: int32 [8], P('groups'), parts along dimension 0, may hold values from 1 to 256, 512 in all
Outputs:
- mamba_out: bfloat16 [1024, 8192], P(('groups', 'seq'), 'dp'), parts along dimension 0
- attn_out: bfloat16 [1024, 4096], P(('groups', 'seq'), 'dp'), parts along dimension 0
There are 2 independent parts, one for each index of `groups`. A program takes and returns all parts, laid end to end along the dimension named above; an argument that names none is the same for every part. Nothing has to cross between parts.
Inputs may be any that keep to these rules, and one draw needn't show every extreme that they name: doc_lens holds 4 document lengths that sum to 512; the longest is exactly 256.
All inputs are finite; a program needn't handle non-finite values.
Results may differ from a plain program's by a relative error of at most 0.018.
Values may be sent and summed in bfloat16 or wider, within the bound.
A program may use at most 128 MiB of HBM per device.

v0:
```python
import functools
import jax
import jax.numpy as jnp
from jax import lax
from jax.experimental import pallas as pl
from jax.experimental.pallas import tpu as pltpu
from jax.sharding import PartitionSpec as P

HDIM = 64
STATE = 128
QHEADS = 32
KVHEADS = 8
ADIM = 128
EPSILON = 1e-05
NEGATIVE = -1e30
LOG2E = 1.4426950408889634
HIGHEST = lax.Precision.HIGHEST
F32 = jnp.float32
BF16 = jnp.bfloat16
CHUNK = 256
NT = (((1,), (1,)), ((), ()))


def silu(value):
    half = 0.5 * value
    return half + half * jnp.tanh(half)


def dot(a, b):
    return jnp.dot(a, b, preferred_element_type=F32)


def wide(tile, width):
    return jnp.concatenate([tile] * (width // tile.shape[1]), axis=1)


def kernel(
    n,
    reach,
    x_hbm, bc_hbm, z_hbm, dt_hbm, cxw_hbm, cxb_hbm, cbw_hbm, cbb_hbm,
    dtb_hbm, alog_hbm, skip_hbm, gain_hbm, q_hbm, k_hbm, v_hbm, lens_hbm,
    mamba_ref,
    attn_ref,
    halo_out,
    halo_in,
    kv,
    state_in,
    state_out,
    xf,
    bcf,
    xc,
    gated,
    gate_entry,
    small_send,
    small_recv,
    kv_send,
    kv_recv,
    st_send,
    st_recv,
    fetch_sem,
    x_tail,
    x_ref, bc_ref, z_ref, dt_ref, cxw_ref, cxb_ref, cbw_ref, cbb_ref,
    dtb_ref, alog_ref, skip_ref, gain_ref, q_ref, k_ref, v_ref, lens_ref,
):
    here = lax.axis_index("seq")
    rows, width = x_ref.shape
    fetches = [
        pltpu.make_async_copy(source, target, fetch_sem.at[i])
        for i, (source, target) in enumerate(
            (
                (x_hbm.at[pl.ds(rows - 16, 16), :], x_tail),
                (bc_hbm, bc_ref),
                (lens_hbm, lens_ref),
                (dt_hbm, dt_ref),
                (dtb_hbm, dtb_ref),
                (alog_hbm, alog_ref),
                (skip_hbm, skip_ref),
                (cbw_hbm, cbw_ref),
                (cbb_hbm, cbb_ref),
                (cxw_hbm, cxw_ref),
                (cxb_hbm, cxb_ref),
                (x_hbm, x_ref),
                (z_hbm, z_ref),
                (k_hbm, k_ref),
                (v_hbm, v_ref),
                (q_hbm, q_ref),
                (gain_hbm, gain_ref),
            )
        )
    ]
    for fetch in fetches:
        fetch.start()
    bc_width = bc_ref.shape[1]
    heads = dt_ref.shape[0]
    groups = bc_width // (2 * STATE)
    chunks = width // CHUNK
    group_width = width // groups
    taps = cxw_ref.shape[0]
    margin = taps - 1
    has_left = here > 0
    has_right = here < n - 1
    right = {"seq": here + 1}

    def remote(src, dst, send, recv):
        return pltpu.make_async_remote_copy(
            src_ref=src,
            dst_ref=dst,
            send_sem=send,
            recv_sem=recv,
            device_id=right,
            device_id_type=pl.DeviceIdType.MESH,
        )

    barrier = pltpu.get_barrier_semaphore()

    @pl.when(has_left)
    def _():
        pl.semaphore_signal(
            barrier, inc=1, device_id={"seq": here - 1}, device_id_type=pl.DeviceIdType.MESH
        )

    @pl.when(has_right)
    def _():
        pl.semaphore_signal(
            barrier, inc=1, device_id={"seq": here + 1}, device_id_type=pl.DeviceIdType.MESH
        )

    fetches[0].wait()
    fetches[1].wait()
    blocks = width // bc_width
    tail_x = x_tail[...].astype(F32)[16 - margin :]
    tail_bc = bc_ref[rows - 16 :, :].astype(F32)[16 - margin :]
    pieces = [tail_x[:, b * bc_width : (b + 1) * bc_width] for b in range(blocks)] + [tail_bc]
    pieces.append(jnp.zeros((16 - margin * (blocks + 1), bc_width), F32))
    halo_out[...] = jnp.concatenate(pieces, axis=0).astype(BF16)

    @pl.when(has_left & has_right)
    def _():
        pl.semaphore_wait(barrier, 2)

    @pl.when(jnp.logical_not(has_left & has_right))
    def _():
        pl.semaphore_wait(barrier, 1)

    halo_copy = remote(halo_out, halo_in, small_send, small_recv)
    own_k = remote(k_hbm, kv.at[0, 0], kv_send.at[0, 0], kv_recv.at[0, 0])
    own_v = remote(v_hbm, kv.at[0, 1], kv_send.at[0, 1], kv_recv.at[0, 1])

    @pl.when(has_right)
    def _():
        halo_copy.start()
        own_k.start()
        own_v.start()

    for fetch in fetches[2:11]:
        fetch.wait()
    first = here * rows
    starts = []
    running_start = jnp.int32(0)
    for d in range(lens_ref.shape[0]):
        starts.append(running_start)
        running_start = running_start + lens_ref[d]

    def doc_of(positions):
        total = jnp.full(positions.shape, -1, jnp.int32)
        for start in starts:
            total = total + jnp.where(start <= positions, 1, 0)
        return total

    square = (rows, 128)
    pos_i = first + lax.broadcasted_iota(jnp.int32, square, 0)
    pos_j = first + lax.broadcasted_iota(jnp.int32, (rows, rows), 1)
    doc_i = doc_of(pos_i)
    doc_j = doc_of(pos_j)
    linked = (doc_i == doc_j) & (pos_i >= pos_j)
    before = doc_of(jnp.full((1, 128), first - 1, jnp.int32))
    last = doc_of(jnp.full((1, 128), first + rows - 1, jnp.int32))
    same = [
        jnp.where(doc_of(pos_i - (margin - lag)) == doc_i, 1.0, 0.0) for lag in range(margin)
    ]

    raw = dt_ref[...].T + dtb_ref[...]
    step = jnp.maximum(raw, 0.0) + jnp.log1p(jnp.exp(-jnp.abs(raw)))
    decay = step * (jnp.exp(alog_ref[...]) * (-LOG2E))
    order_i = lax.broadcasted_iota(jnp.int32, (rows, rows), 0)
    order_j = lax.broadcasted_iota(jnp.int32, (rows, rows), 1)
    lower = jnp.where(order_i >= order_j, 1.0, 0.0)
    running = jnp.dot(lower, decay, precision=HIGHEST, preferred_element_type=F32)
    final = running[rows - 1 : rows]
    row_of = (running - jnp.log2(step)).T
    tail = jnp.where(
        (doc_i == last)[:, :heads], jnp.exp2(final - running) * step, 0.0
    )
    entry = jnp.where((doc_i == before)[:, :heads], jnp.exp2(running), 0.0)
    through = jnp.where((last == before)[:, :heads], jnp.exp2(final), 0.0)
    stack = jnp.concatenate(
        [
            tail,
            entry,
            jnp.broadcast_to(through, (8, heads)),
            jnp.broadcast_to(skip_ref[...], (8, heads)),
        ],
        axis=0,
    )
    high = stack.astype(BF16)
    low = (stack - high.astype(F32)).astype(BF16)

    @pl.when(has_left)
    def _():
        halo_copy.wait_recv()

    @pl.when(here == 0)
    def _():
        halo_in[...] = jnp.zeros_like(halo_in)
        state_in[...] = jnp.zeros_like(state_in)

    for s in range(reach):
        @pl.when(here < s + 1)
        def _(s=s):
            kv[s] = jnp.zeros_like(kv[s])

    halo = halo_in[...].astype(F32)
    for b in range(blocks):
        xf[8 - margin : 8, b * bc_width : (b + 1) * bc_width] = halo[
            b * margin : (b + 1) * margin
        ]
    bcf[8 - margin : 8, :] = halo[blocks * margin : (blocks + 1) * margin]
    bcf[8:, :] = bc_ref[...].astype(F32)

    def conv(source, weight_ref, bias_ref, at, size):
        total = source[8 : 8 + rows, at : at + size] * weight_ref[margin : margin + 1, at : at + size]
        total = total + bias_ref[:, at : at + size]
        for lag in range(margin):
            moved = source[8 - margin + lag : 8 - margin + lag + rows, at : at + size]
            total = total + moved * weight_ref[lag : lag + 1, at : at + size] * wide(
                same[lag], size
            )
        return silu(total).astype(BF16)

    b_turned, c_groups, crossed = [], [], []
    for g in range(groups):
        b_here = conv(bcf, cbw_ref, cbb_ref, 2 * g * STATE, STATE)
        c_here = conv(bcf, cbw_ref, cbb_ref, (2 * g + 1) * STATE, STATE)
        b_turned.append(b_here.astype(F32).T.astype(BF16))
        c_groups.append(c_here)
        crossed.append(lax.dot_general(c_here, b_here, NT, preferred_element_type=F32))

    def state_copy(c):
        return remote(state_out.at[c], state_in.at[c], st_send.at[c], st_recv.at[c])

    lane_head = lax.broadcasted_iota(jnp.int32, (heads, CHUNK), 1) // HDIM
    head_row = lax.broadcasted_iota(jnp.int32, (heads, CHUNK), 0)
    per_chunk = CHUNK // HDIM
    low_half = lax.broadcasted_iota(jnp.int32, (rows, 128), 1) < HDIM

    fetches[11].wait()
    carried = []
    for c in range(chunks):
        at = c * CHUNK
        g = at // group_width
        xf[8:, at : at + CHUNK] = x_ref[:, at : at + CHUNK].astype(F32)
        x_here = conv(xf, cxw_ref, cxb_ref, at, CHUNK)
        xc[:, at : at + CHUNK] = x_here
        spread = jnp.where(head_row == lane_head + c * per_chunk, 1.0, 0.0).astype(BF16)
        expanded = dot(high, spread) + dot(low, spread)
        x32 = x_here.astype(F32)
        local = dot(b_turned[g], (x32 * expanded[:rows]).astype(BF16))
        gate_entry[:, at : at + CHUNK] = expanded[rows : 2 * rows]
        gated[:, at : at + CHUNK] = x32 * expanded[2 * rows + 8 : 2 * rows + 9]
        carried.append(expanded[2 * rows : 2 * rows + 1])
        state_out[c] = local.astype(BF16)

        @pl.when(here == 0)
        def _(c=c):
            state_copy(c).start()

    for s in range(1, reach):
        @pl.when(here >= s)
        def _(s=s):
            for i in range(2):
                remote(
                    kv.at[s - 1, i], kv.at[s - 1, i], kv_send.at[s - 1, i], kv_recv.at[s - 1, i]
                ).wait_recv()

        @pl.when((here >= s) & has_right)
        def _(s=s):
            for i in range(2):
                remote(
                    kv.at[s - 1, i], kv.at[s, i], kv_send.at[s, i], kv_recv.at[s, i]
                ).start()

    for fetch in fetches[12:]:
        fetch.wait()

    kv_local = k_ref.shape[1] // ADIM
    share = q_ref.shape[1] // (ADIM * kv_local)
    scale = ADIM**-0.5 * LOG2E
    key_count = (reach + 1) * rows
    key_pos = (
        first - reach * rows + lax.broadcasted_iota(jnp.int32, (rows, key_count), 1)
    )
    key_docs = doc_of(key_pos)
    permitted = (key_docs == wide(doc_i, key_count)) & (key_pos <= wide(pos_i, key_count))

    def attend(head):
        g = head // share
        cols = slice(g * ADIM, (g + 1) * ADIM)
        keys = jnp.concatenate(
            [kv[s, 0, :, cols] for s in reversed(range(reach))] + [k_ref[:, cols]], axis=0
        )
        values = jnp.concatenate(
            [kv[s, 1, :, cols] for s in reversed(range(reach))] + [v_ref[:, cols]], axis=0
        )
        query = q_ref[:, head * ADIM : (head + 1) * ADIM]
        scores = lax.dot_general(query, keys, NT, preferred_element_type=F32)
        scores = jnp.where(permitted, scores, NEGATIVE)
        peak = jnp.max(scores, axis=1, keepdims=True)
        expo = jnp.exp2((scores - peak) * scale)
        total = jnp.sum(expo, axis=1, keepdims=True)
        summed = dot(expo.astype(BF16), values)
        attn_ref[:, head * ADIM : (head + 1) * ADIM] = (summed / total).astype(BF16)

    q_heads = kv_local * share
    early = chunks // 4
    for c in range(chunks):
        at = c * CHUNK
        g = at // group_width
        gate = silu(z_ref[:, at : at + CHUNK].astype(F32))
        for pair in range(CHUNK // 128):
            col = at + pair * 128
            head = col // HDIM
            parts = []
            for h in (head, head + 1):
                exponent = running[:, h : h + 1] - row_of[h : h + 1, :]
                parts.append(
                    (jnp.exp2(jnp.where(linked, exponent, NEGATIVE)) * crossed[g]).astype(BF16)
                )
            x_pair = xc[:, col : col + 128]
            zero = jnp.zeros_like(x_pair)
            stacked = jnp.concatenate(
                [jnp.where(low_half, x_pair, zero), jnp.where(low_half, zero, x_pair)], axis=0
            )
            inside = dot(jnp.concatenate(parts, axis=1), stacked)
            gated[:, col : col + 128] = (gated[:, col : col + 128] + inside) * gate[
                :, pair * 128 : (pair + 1) * 128
            ]
        gate_entry[:, at : at + CHUNK] = gate_entry[:, at : at + CHUNK] * gate

        @pl.when(has_left)
        def _(c=c):
            state_copy(c).wait_recv()

        @pl.when(has_left & has_right)
        def _(c=c):
            state_out[c] = (
                state_out[c].astype(F32) + state_in[c].astype(F32) * carried[c]
            ).astype(BF16)
            state_copy(c).start()

        if c == early:
            @pl.when(here >= reach)
            def _():
                for i in range(2):
                    remote(
                        kv.at[reach - 1, i],
                        kv.at[reach - 1, i],
                        kv_send.at[reach - 1, i],
                        kv_recv.at[reach - 1, i],
                    ).wait_recv()

        if early <= c < chunks - 1:
            span = chunks - early - 1
            for head in range((c - early) * q_heads // span, (c - early + 1) * q_heads // span):
                attend(head)

        gated[:, at : at + CHUNK] = (
            gated[:, at : at + CHUNK]
            + dot(c_groups[g], state_in[c]) * gate_entry[:, at : at + CHUNK]
        )
        if (at + CHUNK) % group_width == 0:
            left = at + CHUNK - group_width
            value = gated[:, left : left + group_width]
            mean = jnp.sum(value * value, axis=1, keepdims=True) * (1.0 / group_width)
            mamba_ref[:, left : left + group_width] = (
                value * lax.rsqrt(mean + EPSILON) * gain_ref[:, left : left + group_width]
            ).astype(BF16)

    @pl.when(has_right)
    def _():
        halo_copy.wait_send()
        own_k.wait_send()
        own_v.wait_send()
        for c in range(chunks):
            state_copy(c).wait_send()

    for s in range(1, reach):
        @pl.when((here >= s) & has_right)
        def _(s=s):
            for i in range(2):
                remote(
                    kv.at[s - 1, i], kv.at[s, i], kv_send.at[s, i], kv_recv.at[s, i]
                ).wait_send()


def write_out(mamba_ref, attn_ref, mamba_hbm, attn_hbm, sems):
    copies = [
        pltpu.make_async_copy(mamba_ref, mamba_hbm, sems.at[0]),
        pltpu.make_async_copy(attn_ref, attn_hbm, sems.at[1]),
    ]
    for copy in copies:
        copy.start()
    for copy in copies:
        copy.wait()


def shards(n, *args):
    (
        x_raw, bc_raw, z_gate, dt_raw, cxw, cxb, cbw, cbb, dtb, a_log, skip_d, gain, queries, keys,
        values, doc_lens,
    ) = args
    operands = (
        x_raw, bc_raw, z_gate, dt_raw.T, cxw, cxb[None], cbw, cbb[None], dtb[None], a_log[None],
        skip_d[None], gain[None], queries, keys, values, doc_lens,
    )
    rows, width = x_raw.shape
    bc_width = bc_raw.shape[1]
    chunks = width // CHUNK
    reach = max(1, n // 2)
    vmem = pl.BlockSpec(memory_space=pltpu.VMEM)
    dma = pltpu.SemaphoreType.DMA
    results = pl.pallas_call(
        functools.partial(kernel, n, reach),
        out_shape=(pltpu.VMEM((rows, width), BF16), pltpu.VMEM(queries.shape, BF16)),
        in_specs=[pl.BlockSpec(memory_space=pltpu.HBM)] * 16,
        out_specs=(vmem, vmem),
        scratch_shapes=[
            pltpu.VMEM((16, bc_width), BF16),
            pltpu.VMEM((16, bc_width), BF16),
            pltpu.VMEM((reach, 2) + keys.shape, BF16),
            pltpu.VMEM((chunks, STATE, CHUNK), BF16),
            pltpu.VMEM((chunks, STATE, CHUNK), BF16),
            pltpu.VMEM((rows + 8, width), F32),
            pltpu.VMEM((rows + 8, bc_width), F32),
            pltpu.VMEM((rows, width), BF16),
            pltpu.VMEM((rows, width), F32),
            pltpu.VMEM((rows, width), F32),
            dma,
            dma,
            dma((reach, 2)),
            dma((reach, 2)),
            dma((chunks,)),
            dma((chunks,)),
            dma((17,)),
            pltpu.VMEM((16, width), BF16),
        ]
        + [pltpu.VMEM(a.shape, a.dtype) for a in operands[:-1]]
        + [pltpu.SMEM(doc_lens.shape, jnp.int32)],
        compiler_params=pltpu.CompilerParams(
            collective_id=0, has_side_effects=True, vmem_limit_bytes=60 * 1024 * 1024
        ),
    )(*operands)
    hbm = pl.BlockSpec(memory_space=pltpu.HBM)
    return pl.pallas_call(
        write_out,
        out_shape=(
            jax.ShapeDtypeStruct((rows, width), BF16),
            jax.ShapeDtypeStruct(queries.shape, BF16),
        ),
        in_specs=[vmem, vmem],
        out_specs=(hbm, hbm),
        scratch_shapes=[dma((2,))],
    )(*[pltpu.with_memory_space_constraint(r, pltpu.VMEM) for r in results])


def solution(mesh):
    both = P(("groups", "seq"), "dp")
    placed = (
        both, both, both, both, P(None, "dp"), P("dp"), P(None, "dp"), P("dp"), P("dp"), P("dp"),
        P("dp"), P("dp"), both, both, both, P("groups"),
    )
    return jax.shard_map(
        functools.partial(shards, mesh.shape["seq"]),
        mesh=mesh,
        in_specs=placed,
        out_specs=(both, both),
        check_vma=False,
    )
```

profile of v0, /device:TPU:26, one launch (start us, length us, event | category | flops | bytes accessed | tf_op | source)
XLA Modules:
  0.0 26.1 jit_solution(7858625010467778892)
XLA Ops:
  0.6 24.6 %shard_map.167 = (bf16[128,2048]{1,0:T(8,128)(2,1)S(1)}, bf16[128,1024]{1,0:T(8,128)(2,1)S(1)}) custom-call(bf16[128,2048]{1,0:T(8,128)(2,1)} %x_hbm.1, bf16[128,512]{1,0:T(8,128)(2,1)} %bc_hbm.1, bf16[128,2048]{1,0:T(8,128)(2,1)} %z_hbm.1, f32[32,128]{1,0:T(8,128)} %bitcast.7, f32[4,2048]{1,0:T(4,128)} %cxw_hbm.1, f32[1,2048]{1,0:T(1,128)} %bitcast.8, ...), custom_call_target="tpu_custom_call" | custom-call | tf_op jit(solution)/shard_map/pallas_call | solution.py:431
  25.2 0.9 %shard_map.168 = (bf16[128,2048]{1,0:T(8,128)(2,1)}, bf16[128,1024]{1,0:T(8,128)(2,1)}) custom-call(bf16[128,2048]{1,0:T(8,128)(2,1)S(1)} %get-tuple-element.4.mamba_ref, bf16[128,1024]{1,0:T(8,128)(2,1)S(1)} %get-tuple-element.5.attn_ref), custom_call_target="tpu_custom_call" | custom-call | tf_op jit(solution)/shard_map/pallas_call | solution.py:463
where the time goes:
time: 26.2 us; the launch traced here: 26.1 us
  Pallas kernels  25.5 us (97%)
  between operations  0.64 us (2%)
    pallas_call x1, Pallas kernels, shards(): pl.pallas_call(functools.partial(kernel, n, reach), out_shape=(pltpu.VMEM...  24.6 us
    pallas_call x1, Pallas kernels, shards(): pl.pallas_call(write_out, out_shape=(jax.ShapeDtypeStruct((rows, width),...  0.89 us

commit v1 on v0

--- a/solution.py
+++ b/solution.py
@@ -34,7 +34,7 @@
     return jnp.concatenate([tile] * (width // tile.shape[1]), axis=1)
 
 
-def kernel(
+def relay_kernel(
     n,
     reach,
     x_hbm, bc_hbm, z_hbm, dt_hbm, cxw_hbm, cxb_hbm, cbw_hbm, cbb_hbm,
@@ -402,6 +402,404 @@
                 ).wait_send()
 
 
+SUB = 128
+
+
+def packed_kernel(
+    n,
+    x_hbm, bc_hbm, z_hbm, dt_hbm, cxw_hbm, cxb_hbm, cbw_hbm, cbb_hbm,
+    dtb_hbm, alog_hbm, skip_hbm, gain_hbm, q_hbm, k_hbm, v_hbm, lens_hbm,
+    mamba_ref,
+    attn_ref,
+    halo_out,
+    halo_in,
+    kv,
+    state_in,
+    state_out,
+    c_mine,
+    c_next,
+    xf,
+    bcf,
+    xc,
+    gated,
+    gate_entry,
+    small_send,
+    small_recv,
+    kv_send,
+    kv_recv,
+    st_send,
+    st_recv,
+    c_sem,
+    fetch_sem,
+    x_tail,
+    x_ref, bc_ref, z_ref, dt_ref, cxw_ref, cxb_ref, cbw_ref, cbb_ref,
+    dtb_ref, alog_ref, skip_ref, gain_ref, q_ref, k_ref, v_ref, lens_ref,
+):
+    here = lax.axis_index("seq")
+    rows, width = x_ref.shape
+    fetches = [
+        pltpu.make_async_copy(source, target, fetch_sem.at[i])
+        for i, (source, target) in enumerate(
+            (
+                (x_hbm.at[pl.ds(rows - 16, 16), :], x_tail),
+                (bc_hbm, bc_ref),
+                (lens_hbm, lens_ref),
+                (dt_hbm, dt_ref),
+                (dtb_hbm, dtb_ref),
+                (alog_hbm, alog_ref),
+                (skip_hbm, skip_ref),
+                (cbw_hbm, cbw_ref),
+                (cbb_hbm, cbb_ref),
+                (cxw_hbm, cxw_ref),
+                (cxb_hbm, cxb_ref),
+                (x_hbm, x_ref),
+                (z_hbm, z_ref),
+                (k_hbm, k_ref),
+                (v_hbm, v_ref),
+                (q_hbm, q_ref),
+                (gain_hbm, gain_ref),
+            )
+        )
+    ]
+    for fetch in fetches:
+        fetch.start()
+    bc_width = bc_ref.shape[1]
+    heads = dt_ref.shape[0]
+    groups = bc_width // (2 * STATE)
+    chunks = width // CHUNK
+    per = CHUNK // SUB
+    group_width = width // groups
+    taps = cxw_ref.shape[0]
+    margin = taps - 1
+    has_left = here > 0
+    has_right = here < n - 1
+    middle = has_left & has_right
+
+    def remote(src, dst, send, recv, to=1):
+        return pltpu.make_async_remote_copy(
+            src_ref=src,
+            dst_ref=dst,
+            send_sem=send,
+            recv_sem=recv,
+            device_id={"seq": here + to},
+            device_id_type=pl.DeviceIdType.MESH,
+        )
+
+    barrier = pltpu.get_barrier_semaphore()
+
+    @pl.when(has_left)
+    def _():
+        pl.semaphore_signal(
+            barrier, inc=1, device_id={"seq": here - 1}, device_id_type=pl.DeviceIdType.MESH
+        )
+
+    @pl.when(has_right)
+    def _():
+        pl.semaphore_signal(
+            barrier, inc=1, device_id={"seq": here + 1}, device_id_type=pl.DeviceIdType.MESH
+        )
+
+    fetches[0].wait()
+    fetches[1].wait()
+    blocks = width // bc_width
+    tail_x = x_tail[...].astype(F32)[16 - margin :]
+    tail_bc = bc_ref[rows - 16 :, :].astype(F32)[16 - margin :]
+    pieces = [tail_x[:, b * bc_width : (b + 1) * bc_width] for b in range(blocks)] + [tail_bc]
+    pieces.append(jnp.zeros((16 - margin * (blocks + 1), bc_width), F32))
+    halo_out[...] = jnp.concatenate(pieces, axis=0).astype(BF16)
+
+    @pl.when(middle)
+    def _():
+        pl.semaphore_wait(barrier, 2)
+
+    @pl.when(jnp.logical_not(middle))
+    def _():
+        pl.semaphore_wait(barrier, 1)
+
+    halo_copy = remote(halo_out, halo_in, small_send, small_recv)
+    own_k = remote(k_hbm, kv.at[0], kv_send.at[0], kv_recv.at[0])
+    own_v = remote(v_hbm, kv.at[1], kv_send.at[1], kv_recv.at[1])
+    c_back = remote(c_mine, c_next, c_sem.at[0], c_sem.at[1], -1)
+
+    @pl.when(has_right)
+    def _():
+        halo_copy.start()
+        own_k.start()
+        own_v.start()
+
+    for fetch in fetches[2:11]:
+        fetch.wait()
+    first = here * rows
+    starts = []
+    running_start = jnp.int32(0)
+    for d in range(lens_ref.shape[0]):
+        starts.append(running_start)
+        running_start = running_start + lens_ref[d]
+
+    def doc_of(positions):
+        total = jnp.full(positions.shape, -1, jnp.int32)
+        for start in starts:
+            total = total + jnp.where(start <= positions, 1, 0)
+        return total
+
+    def doc_at(position):
+        return doc_of(jnp.full((1, 128), position, jnp.int32))
+
+    square = (rows, 128)
+    pos_i = first + lax.broadcasted_iota(jnp.int32, square, 0)
+    pos_j = first + lax.broadcasted_iota(jnp.int32, (rows, rows), 1)
+    doc_i = doc_of(pos_i)
+    doc_j = doc_of(pos_j)
+    linked = (doc_i == doc_j) & (pos_i >= pos_j)
+    before = doc_at(first - 1)
+    last = doc_at(first + rows - 1)
+    same = [
+        jnp.where(doc_of(pos_i - (margin - lag)) == doc_i, 1.0, 0.0) for lag in range(margin)
+    ]
+    ahead = doc_of(pos_i + rows) == before
+    spare = (doc_at(first + rows) == before) & jnp.logical_not(ahead)
+    rows_came = doc_at(first - rows - 1) == doc_at(first)
+
+    raw = dt_ref[...].T + dtb_ref[...]
+    step = jnp.maximum(raw, 0.0) + jnp.log1p(jnp.exp(-jnp.abs(raw)))
+    decay = step * (jnp.exp(alog_ref[...]) * (-LOG2E))
+    order_i = lax.broadcasted_iota(jnp.int32, (rows, rows), 0)
+    order_j = lax.broadcasted_iota(jnp.int32, (rows, rows), 1)
+    unit = jnp.where(order_i == order_j, 1.0, 0.0)
+    lower = jnp.where(order_i >= order_j, 1.0, 0.0)
+    running = jnp.dot(lower, decay, precision=HIGHEST, preferred_element_type=F32)
+    final = running[rows - 1 : rows]
+    row_of = (running - jnp.log2(step)).T
+    tail = jnp.where(
+        (doc_i == last)[:, :heads], jnp.exp2(final - running) * step, 0.0
+    )
+    entry = jnp.where((doc_i == before)[:, :heads], jnp.exp2(running), 0.0)
+    through = jnp.where((last == before)[:, :heads], jnp.exp2(final), 0.0)
+    stack = jnp.concatenate(
+        [
+            tail,
+            entry,
+            jnp.broadcast_to(through, (8, heads)),
+            jnp.broadcast_to(skip_ref[...], (8, heads)),
+        ],
+        axis=0,
+    )
+    high = stack.astype(BF16)
+    low = (stack - high.astype(F32)).astype(BF16)
+
+    @pl.when(has_left)
+    def _():
+        halo_copy.wait_recv()
+
+    @pl.when(here == 0)
+    def _():
+        halo_in[...] = jnp.zeros_like(halo_in)
+        state_in[...] = jnp.zeros_like(state_in)
+        kv[...] = jnp.zeros_like(kv)
+
+    halo = halo_in[...].astype(F32)
+    for b in range(blocks):
+        xf[8 - margin : 8, b * bc_width : (b + 1) * bc_width] = halo[
+            b * margin : (b + 1) * margin
+        ]
+    bcf[8 - margin : 8, :] = halo[blocks * margin : (blocks + 1) * margin]
+    bcf[8:, :] = bc_ref[...].astype(F32)
+
+    def conv(source, weight_ref, bias_ref, at, size):
+        total = source[8 : 8 + rows, at : at + size] * weight_ref[margin : margin + 1, at : at + size]
+        total = total + bias_ref[:, at : at + size]
+        for lag in range(margin):
+            moved = source[8 - margin + lag : 8 - margin + lag + rows, at : at + size]
+            total = total + moved * weight_ref[lag : lag + 1, at : at + size] * wide(
+                same[lag], size
+            )
+        return silu(total).astype(BF16)
+
+    b_turned, c_groups, crossed = [], [], []
+    for g in range(groups):
+        b_here = conv(bcf, cbw_ref, cbb_ref, 2 * g * STATE, STATE)
+        c_here = conv(bcf, cbw_ref, cbb_ref, (2 * g + 1) * STATE, STATE)
+        b_turned.append(b_here.astype(F32).T.astype(BF16))
+        c_mine[g] = c_here
+        c_groups.append(jnp.where(rows_came, unit, c_here.astype(F32)).astype(BF16))
+        crossed.append(lax.dot_general(c_here, b_here, NT, preferred_element_type=F32))
+
+    @pl.when(here >= 2)
+    def _():
+        c_back.start()
+
+    def state_copy(i):
+        return remote(state_out.at[i], state_in.at[i], st_send.at[i], st_recv.at[i])
+
+    kv_local = k_ref.shape[1] // ADIM
+    lane_head = lax.broadcasted_iota(jnp.int32, (heads, CHUNK), 1) // HDIM
+    head_row = lax.broadcasted_iota(jnp.int32, (heads, CHUNK), 0)
+    per_chunk = CHUNK // HDIM
+    low_half = lax.broadcasted_iota(jnp.int32, (rows, 128), 1) < HDIM
+    carried = []
+
+    def make_local(c):
+        at = c * CHUNK
+        g = at // group_width
+        xf[8:, at : at + CHUNK] = x_ref[:, at : at + CHUNK].astype(F32)
+        x_here = conv(xf, cxw_ref, cxb_ref, at, CHUNK)
+        xc[:, at : at + CHUNK] = x_here
+        spread = jnp.where(head_row == lane_head + c * per_chunk, 1.0, 0.0).astype(BF16)
+        expanded = dot(high, spread) + dot(low, spread)
+        x32 = x_here.astype(F32)
+        local = dot(b_turned[g], (x32 * expanded[:rows]).astype(BF16)).astype(BF16)
+        gate_entry[:, at : at + CHUNK] = expanded[rows : 2 * rows]
+        gated[:, at : at + CHUNK] = x32 * expanded[2 * rows + 8 : 2 * rows + 9]
+        carried.append(expanded[2 * rows : 2 * rows + 1])
+        for i in range(per):
+            state_out[c * per + i] = local[:, i * SUB : (i + 1) * SUB]
+
+        @pl.when(here == 0)
+        def _():
+            for i in range(per):
+                state_copy(c * per + i).start()
+
+    def pass_on(c):
+        g = c * CHUNK // group_width
+
+        @pl.when(middle)
+        def _():
+            for i in range(per):
+                at = c * per + i
+                state_copy(at).wait_recv()
+                state = state_out[at].astype(F32) + state_in[at].astype(F32) * carried[c][
+                    :, i * SUB : (i + 1) * SUB
+                ]
+                sent = dot(c_next[g], state.astype(BF16))
+                if at < 2 * kv_local:
+                    col = at % kv_local * ADIM
+                    sent = jnp.where(
+                        spare, kv[at // kv_local, :, col : col + ADIM].astype(F32), sent
+                    )
+                state_out[at] = sent.astype(BF16)
+                state_copy(at).start()
+
+    def arrive(c):
+        @pl.when(here == n - 1)
+        def _():
+            for i in range(per):
+                state_copy(c * per + i).wait_recv()
+
+    share = q_ref.shape[1] // (ADIM * kv_local)
+    q_heads = kv_local * share
+    scale = ADIM**-0.5 * LOG2E
+
+    def permitted_keys():
+        count = 3 * rows
+        key_pos = first - 2 * rows + lax.broadcasted_iota(jnp.int32, (rows, count), 1)
+        return (doc_of(key_pos) == wide(doc_i, count)) & (key_pos <= wide(pos_i, count))
+
+    def attend(head, permitted):
+        g = head // share
+        cols = slice(g * ADIM, (g + 1) * ADIM)
+        keys = jnp.concatenate([state_in[g], kv[0, :, cols], k_ref[:, cols]], axis=0)
+        values = jnp.concatenate([state_in[kv_local + g], kv[1, :, cols], v_ref[:, cols]], axis=0)
+        query = q_ref[:, head * ADIM : (head + 1) * ADIM]
+        scores = lax.dot_general(query, keys, NT, preferred_element_type=F32)
+        scores = jnp.where(permitted, scores, NEGATIVE)
+        peak = jnp.max(scores, axis=1, keepdims=True)
+        expo = jnp.exp2((scores - peak) * scale)
+        total = jnp.sum(expo, axis=1, keepdims=True)
+        summed = dot(expo.astype(BF16), values)
+        attn_ref[:, head * ADIM : (head + 1) * ADIM] = (summed / total).astype(BF16)
+
+    def inside(c):
+        at = c * CHUNK
+        g = at // group_width
+        gate = silu(z_ref[:, at : at + CHUNK].astype(F32))
+        for pair in range(CHUNK // 128):
+            col = at + pair * 128
+            head = col // HDIM
+            parts = []
+            for h in (head, head + 1):
+                exponent = running[:, h : h + 1] - row_of[h : h + 1, :]
+                parts.append(
+                    (jnp.exp2(jnp.where(linked, exponent, NEGATIVE)) * crossed[g]).astype(BF16)
+                )
+            x_pair = xc[:, col : col + 128]
+            zero = jnp.zeros_like(x_pair)
+            stacked = jnp.concatenate(
+                [jnp.where(low_half, x_pair, zero), jnp.where(low_half, zero, x_pair)], axis=0
+            )
+            within = dot(jnp.concatenate(parts, axis=1), stacked)
+            gated[:, col : col + 128] = (gated[:, col : col + 128] + within) * gate[
+                :, pair * 128 : (pair + 1) * 128
+            ]
+        gate_entry[:, at : at + CHUNK] = gate_entry[:, at : at + CHUNK] * gate
+
+    def finish(c):
+        at = c * CHUNK
+        g = at // group_width
+        came = jnp.concatenate([state_in[c * per + i] for i in range(per)], axis=1)
+        gated[:, at : at + CHUNK] = (
+            gated[:, at : at + CHUNK]
+            + dot(c_groups[g], came) * gate_entry[:, at : at + CHUNK]
+        )
+        if (at + CHUNK) % group_width == 0:
+            left = at + CHUNK - group_width
+            value = gated[:, left : left + group_width]
+            mean = jnp.sum(value * value, axis=1, keepdims=True) * (1.0 / group_width)
+            mamba_ref[:, left : left + group_width] = (
+                value * lax.rsqrt(mean + EPSILON) * gain_ref[:, left : left + group_width]
+            ).astype(BF16)
+
+    fetches[11].wait()
+    lag = chunks // 2
+    for c in range(chunks):
+        make_local(c)
+        if c == lag - 1:
+            @pl.when(has_left)
+            def _():
+                own_k.wait_recv()
+                own_v.wait_recv()
+
+            @pl.when(middle)
+            def _():
+                c_back.wait_recv()
+                for g in range(groups):
+                    c_next[g] = jnp.where(ahead, c_next[g].astype(F32), unit).astype(BF16)
+        if c >= lag:
+            pass_on(c - lag)
+
+    for fetch in fetches[12:]:
+        fetch.wait()
+    left_over = list(range(chunks - lag, chunks))
+    for c in range(chunks):
+        inside(c)
+        if c % 4 == 1 and len(left_over) > 2:
+            pass_on(left_over.pop(0))
+    arrive(0)
+    arrive(1)
+    permitted = permitted_keys()
+    for head in range(q_heads):
+        attend(head, permitted)
+        if head % 4 == 3 and left_over:
+            pass_on(left_over.pop(0))
+    for c in left_over:
+        pass_on(c)
+    for c in range(chunks):
+        if c > 1:
+            arrive(c)
+        finish(c)
+
+    @pl.when(has_right)
+    def _():
+        halo_copy.wait_send()
+        own_k.wait_send()
+        own_v.wait_send()
+        for i in range(chunks * per):
+            state_copy(i).wait_send()
+
+    @pl.when(here >= 2)
+    def _():
+        c_back.wait_send()
+
+
 def write_out(mamba_ref, attn_ref, mamba_hbm, attn_hbm, sems):
     copies = [
         pltpu.make_async_copy(mamba_ref, mamba_hbm, sems.at[0]),
@@ -428,17 +826,29 @@
     reach = max(1, n // 2)
     vmem = pl.BlockSpec(memory_space=pltpu.VMEM)
     dma = pltpu.SemaphoreType.DMA
+    if reach == 2 and rows == STATE and keys.shape[1] == CHUNK and 2 * CHUNK <= width:
+        subs = width // SUB
+        state = pltpu.VMEM((subs, STATE, SUB), BF16)
+        turned = pltpu.VMEM((bc_width // (2 * STATE), rows, STATE), BF16)
+        body = functools.partial(packed_kernel, n)
+        buffers = [pltpu.VMEM((2,) + keys.shape, BF16), state, state, turned, turned]
+        sems = [dma((2,)), dma((2,)), dma((subs,)), dma((subs,)), dma((2,))]
+    else:
+        state = pltpu.VMEM((chunks, STATE, CHUNK), BF16)
+        body = functools.partial(relay_kernel, n, reach)
+        buffers = [pltpu.VMEM((reach, 2) + keys.shape, BF16), state, state]
+        sems = [dma((reach, 2)), dma((reach, 2)), dma((chunks,)), dma((chunks,))]
     results = pl.pallas_call(
-        functools.partial(kernel, n, reach),
+        body,
         out_shape=(pltpu.VMEM((rows, width), BF16), pltpu.VMEM(queries.shape, BF16)),
         in_specs=[pl.BlockSpec(memory_space=pltpu.HBM)] * 16,
         out_specs=(vmem, vmem),
         scratch_shapes=[
             pltpu.VMEM((16, bc_width), BF16),
             pltpu.VMEM((16, bc_width), BF16),
-            pltpu.VMEM((reach, 2) + keys.shape, BF16),
-            pltpu.VMEM((chunks, STATE, CHUNK), BF16),
-            pltpu.VMEM((chunks, STATE, CHUNK), BF16),
+        ]
+        + buffers
+        + [
             pltpu.VMEM((rows + 8, width), F32),
             pltpu.VMEM((rows + 8, bc_width), F32),
             pltpu.VMEM((rows, width), BF16),
@@ -446,13 +856,9 @@
             pltpu.VMEM((rows, width), F32),
             dma,
             dma,
-            dma((reach, 2)),
-            dma((reach, 2)),
-            dma((chunks,)),
-            dma((chunks,)),
-            dma((17,)),
-            pltpu.VMEM((16, width), BF16),
         ]
+        + sems
+        + [dma((17,)), pltpu.VMEM((16, width), BF16)]
         + [pltpu.VMEM(a.shape, a.dtype) for a in operands[:-1]]
         + [pltpu.SMEM(doc_lens.shape, jnp.int32)],
         compiler_params=pltpu.CompilerParams(

time: 26.2 us -> 26.4 us (level)
  no operation moved by 1% of the time
where the time goes in v1:
time: 26.4 us; the launch traced here: 26.3 us
  Pallas kernels  25.6 us (97%)
  between operations  0.64 us (2%)
    pallas_call x1, Pallas kernels, shards(): pl.pallas_call(body, out_shape=(pltpu.VMEM((rows, width), BF16), pltpu.VM...  24.7 us
    pallas_call x1, Pallas kernels, shards(): pl.pallas_call(write_out, out_shape=(jax.ShapeDtypeStruct((rows, width),...  0.89 us

profile of v1, /device:TPU:26, one launch (start us, length us, event | category | flops | bytes accessed | tf_op | source)
XLA Modules:
  0.0 26.3 jit_solution(12107499080373990651)
XLA Ops:
  0.6 24.7 %shard_map.167 = (bf16[128,2048]{1,0:T(8,128)(2,1)S(1)}, bf16[128,1024]{1,0:T(8,128)(2,1)S(1)}) custom-call(bf16[128,2048]{1,0:T(8,128)(2,1)} %x_hbm.1, bf16[128,512]{1,0:T(8,128)(2,1)} %bc_hbm.1, bf16[128,2048]{1,0:T(8,128)(2,1)} %z_hbm.1, f32[32,128]{1,0:T(8,128)} %bitcast.7, f32[4,2048]{1,0:T(4,128)} %cxw_hbm.1, f32[1,2048]{1,0:T(1,128)} %bitcast.8, ...), custom_call_target="tpu_custom_call" | custom-call | tf_op jit(solution)/shard_map/pallas_call | solution.py:841
  25.4 0.9 %shard_map.168 = (bf16[128,2048]{1,0:T(8,128)(2,1)}, bf16[128,1024]{1,0:T(8,128)(2,1)}) custom-call(bf16[128,2048]{1,0:T(8,128)(2,1)S(1)} %get-tuple-element.4.mamba_ref, bf16[128,1024]{1,0:T(8,128)(2,1)S(1)} %get-tuple-element.5.attn_ref), custom_call_target="tpu_custom_call" | custom-call | tf_op jit(solution)/shard_map/pallas_call | solution.py:869

commit v2 on v1

--- a/solution.py
+++ b/solution.py
@@ -403,6 +403,38 @@
 
 
 SUB = 128
+ORDER = (
+    ("l", 0, 6),
+    ("k", 0, 1),
+    ("t", 0, 1),
+    ("l", 6, 8),
+    ("p", 0, 1),
+    ("w", 0, 1),
+    ("i", 0, 4),
+    ("p", 1, 2),
+    ("i", 4, 8),
+    ("p", 2, 3),
+    ("r", 0, 2),
+    ("a", 0, 3),
+    ("p", 3, 4),
+    ("a", 3, 6),
+    ("p", 4, 5),
+    ("a", 6, 8),
+    ("p", 5, 8),
+    ("f", 0, 2),
+    ("r", 2, 3),
+    ("f", 2, 3),
+    ("r", 3, 4),
+    ("f", 3, 4),
+    ("r", 4, 5),
+    ("f", 4, 5),
+    ("r", 5, 6),
+    ("f", 5, 6),
+    ("r", 6, 7),
+    ("f", 6, 7),
+    ("r", 7, 8),
+    ("f", 7, 8),
+)
 
 
 def packed_kernel(
@@ -749,43 +781,38 @@
             ).astype(BF16)
 
     fetches[11].wait()
-    lag = chunks // 2
-    for c in range(chunks):
-        make_local(c)
-        if c == lag - 1:
-            @pl.when(has_left)
-            def _():
-                own_k.wait_recv()
-                own_v.wait_recv()
-
-            @pl.when(middle)
-            def _():
-                c_back.wait_recv()
-                for g in range(groups):
-                    c_next[g] = jnp.where(ahead, c_next[g].astype(F32), unit).astype(BF16)
-        if c >= lag:
-            pass_on(c - lag)
-
-    for fetch in fetches[12:]:
-        fetch.wait()
-    left_over = list(range(chunks - lag, chunks))
-    for c in range(chunks):
-        inside(c)
-        if c % 4 == 1 and len(left_over) > 2:
-            pass_on(left_over.pop(0))
-    arrive(0)
-    arrive(1)
-    permitted = permitted_keys()
-    for head in range(q_heads):
-        attend(head, permitted)
-        if head % 4 == 3 and left_over:
-            pass_on(left_over.pop(0))
-    for c in left_over:
-        pass_on(c)
-    for c in range(chunks):
-        if c > 1:
-            arrive(c)
-        finish(c)
+
+    def take_keys():
+        @pl.when(has_left)
+        def _():
+            own_k.wait_recv()
+            own_v.wait_recv()
+
+    def take_turned():
+        @pl.when(middle)
+        def _():
+            c_back.wait_recv()
+            for g in range(groups):
+                c_next[g] = jnp.where(ahead, c_next[g].astype(F32), unit).astype(BF16)
+
+    def take_rest():
+        for fetch in fetches[12:]:
+            fetch.wait()
+
+    held = []
+
+    def attend_next(head):
+        if not held:
+            held.append(permitted_keys())
+        attend(head, held[0])
+
+    steps = {
+        "l": make_local, "p": pass_on, "r": arrive, "i": inside, "a": attend_next, "f": finish,
+        "k": lambda _: take_keys(), "t": lambda _: take_turned(), "w": lambda _: take_rest(),
+    }
+    for name, low_end, high_end in ORDER:
+        for at in range(low_end, high_end):
+            steps[name](at)
 
     @pl.when(has_right)
     def _():
@@ -826,7 +853,9 @@
     reach = max(1, n // 2)
     vmem = pl.BlockSpec(memory_space=pltpu.VMEM)
     dma = pltpu.SemaphoreType.DMA
-    if reach == 2 and rows == STATE and keys.shape[1] == CHUNK and 2 * CHUNK <= width:
+    if reach == 2 and rows == STATE and keys.shape[1] == CHUNK and width == 8 * CHUNK and (
+        queries.shape[1] == 8 * ADIM
+    ):
         subs = width // SUB
         state = pltpu.VMEM((subs, STATE, SUB), BF16)
         turned = pltpu.VMEM((bc_width // (2 * STATE), rows, STATE), BF16)

time: 26.4 us -> 25.2 us (0.955)
  Pallas kernels: 25.6 us -> 24.4 us
    pallas_call x1, Pallas kernels: 24.7 us -> 23.5 us  [shards(): pl.pallas_call(body, out_shape=(pltpu.VMEM((rows, width), BF16), pltpu.VM...]
where the time goes in v2:
time: 25.2 us; the launch traced here: 25 us
  Pallas kernels  24.4 us (97%)
  between operations  0.64 us (3%)
    pallas_call x1, Pallas kernels, shards(): pl.pallas_call(body, out_shape=(pltpu.VMEM((rows, width), BF16), pltpu.VM...  23.5 us
    pallas_call x1, Pallas kernels, shards(): pl.pallas_call(write_out, out_shape=(jax.ShapeDtypeStruct((rows, width),...  0.89 us

profile of v2, /device:TPU:26, one launch (start us, length us, event | category | flops | bytes accessed | tf_op | source)
XLA Modules:
  0.0 25.0 jit_solution(3569964474904847342)
XLA Ops:
  0.6 23.5 %shard_map.167 = (bf16[128,2048]{1,0:T(8,128)(2,1)S(1)}, bf16[128,1024]{1,0:T(8,128)(2,1)S(1)}) custom-call(bf16[128,2048]{1,0:T(8,128)(2,1)} %x_hbm.1, bf16[128,512]{1,0:T(8,128)(2,1)} %bc_hbm.1, bf16[128,2048]{1,0:T(8,128)(2,1)} %z_hbm.1, f32[32,128]{1,0:T(8,128)} %bitcast.7, f32[4,2048]{1,0:T(4,128)} %cxw_hbm.1, f32[1,2048]{1,0:T(1,128)} %bitcast.8, ...), custom_call_target="tpu_custom_call" | custom-call | tf_op jit(solution)/shard_map/pallas_call | solution.py:870
  24.1 0.9 %shard_map.168 = (bf16[128,2048]{1,0:T(8,128)(2,1)}, bf16[128,1024]{1,0:T(8,128)(2,1)}) custom-call(bf16[128,2048]{1,0:T(8,128)(2,1)S(1)} %get-tuple-element.4.mamba_ref, bf16[128,1024]{1,0:T(8,128)(2,1)S(1)} %get-tuple-element.5.attn_ref), custom_call_target="tpu_custom_call" | custom-call | tf_op jit(solution)/shard_map/pallas_call | solution.py:898

commit v3 on v2

--- a/solution.py
+++ b/solution.py
@@ -404,10 +404,14 @@
 
 SUB = 128
 ORDER = (
-    ("l", 0, 6),
+    ("l", 7, 8),
+    ("e", 0, 1),
+    ("l", 0, 7),
+    ("o", 0, 1),
     ("k", 0, 1),
     ("t", 0, 1),
-    ("l", 6, 8),
+    ("q", 0, 4),
+    ("x", 0, 1),
     ("p", 0, 1),
     ("w", 0, 1),
     ("i", 0, 4),
@@ -420,20 +424,23 @@
     ("a", 3, 6),
     ("p", 4, 5),
     ("a", 6, 8),
-    ("p", 5, 8),
+    ("p", 5, 7),
     ("f", 0, 2),
     ("r", 2, 3),
     ("f", 2, 3),
     ("r", 3, 4),
     ("f", 3, 4),
+    ("n", 0, 1),
+    ("y", 0, 1),
     ("r", 4, 5),
     ("f", 4, 5),
     ("r", 5, 6),
     ("f", 5, 6),
+    ("r", 7, 8),
+    ("f", 7, 8),
     ("r", 6, 7),
     ("f", 6, 7),
-    ("r", 7, 8),
-    ("f", 7, 8),
+    ("n", 1, 2),
 )
 
 
@@ -450,6 +457,9 @@
     state_out,
     c_mine,
     c_next,
+    c_ahead,
+    ready,
+    extra,
     xf,
     bcf,
     xc,
@@ -462,12 +472,30 @@
     st_send,
     st_recv,
     c_sem,
+    extra_sem,
     fetch_sem,
     x_tail,
     x_ref, bc_ref, z_ref, dt_ref, cxw_ref, cxb_ref, cbw_ref, cbb_ref,
     dtb_ref, alog_ref, skip_ref, gain_ref, q_ref, k_ref, v_ref, lens_ref,
 ):
     here = lax.axis_index("seq")
+    has_left = here > 0
+    has_right = here < n - 1
+    middle = has_left & has_right
+    barrier = pltpu.get_barrier_semaphore()
+
+    @pl.when(has_left)
+    def _():
+        pl.semaphore_signal(
+            barrier, inc=1, device_id={"seq": here - 1}, device_id_type=pl.DeviceIdType.MESH
+        )
+
+    @pl.when(has_right)
+    def _():
+        pl.semaphore_signal(
+            barrier, inc=1, device_id={"seq": here + 1}, device_id_type=pl.DeviceIdType.MESH
+        )
+
     rows, width = x_ref.shape
     fetches = [
         pltpu.make_async_copy(source, target, fetch_sem.at[i])
@@ -503,9 +531,6 @@
     group_width = width // groups
     taps = cxw_ref.shape[0]
     margin = taps - 1
-    has_left = here > 0
-    has_right = here < n - 1
-    middle = has_left & has_right
 
     def remote(src, dst, send, recv, to=1):
         return pltpu.make_async_remote_copy(
@@ -515,20 +540,6 @@
             recv_sem=recv,
             device_id={"seq": here + to},
             device_id_type=pl.DeviceIdType.MESH,
-        )
-
-    barrier = pltpu.get_barrier_semaphore()
-
-    @pl.when(has_left)
-    def _():
-        pl.semaphore_signal(
-            barrier, inc=1, device_id={"seq": here - 1}, device_id_type=pl.DeviceIdType.MESH
-        )
-
-    @pl.when(has_right)
-    def _():
-        pl.semaphore_signal(
-            barrier, inc=1, device_id={"seq": here + 1}, device_id_type=pl.DeviceIdType.MESH
         )
 
     fetches[0].wait()
@@ -629,6 +640,10 @@
         state_in[...] = jnp.zeros_like(state_in)
         kv[...] = jnp.zeros_like(kv)
 
+    @pl.when(here != 2)
+    def _():
+        extra[...] = jnp.zeros_like(extra)
+
     halo = halo_in[...].astype(F32)
     for b in range(blocks):
         xf[8 - margin : 8, b * bc_width : (b + 1) * bc_width] = halo[
@@ -647,12 +662,13 @@
             )
         return silu(total).astype(BF16)
 
-    b_turned, c_groups, crossed = [], [], []
+    b_turned, c_groups, crossed, c_own = [], [], [], []
     for g in range(groups):
         b_here = conv(bcf, cbw_ref, cbb_ref, 2 * g * STATE, STATE)
         c_here = conv(bcf, cbw_ref, cbb_ref, (2 * g + 1) * STATE, STATE)
         b_turned.append(b_here.astype(F32).T.astype(BF16))
         c_mine[g] = c_here
+        c_own.append(c_here)
         c_groups.append(jnp.where(rows_came, unit, c_here.astype(F32)).astype(BF16))
         crossed.append(lax.dot_general(c_here, b_here, NT, preferred_element_type=F32))
 
@@ -668,7 +684,7 @@
     head_row = lax.broadcasted_iota(jnp.int32, (heads, CHUNK), 0)
     per_chunk = CHUNK // HDIM
     low_half = lax.broadcasted_iota(jnp.int32, (rows, 128), 1) < HDIM
-    carried = []
+    carried = {}
 
     def make_local(c):
         at = c * CHUNK
@@ -682,14 +698,71 @@
         local = dot(b_turned[g], (x32 * expanded[:rows]).astype(BF16)).astype(BF16)
         gate_entry[:, at : at + CHUNK] = expanded[rows : 2 * rows]
         gated[:, at : at + CHUNK] = x32 * expanded[2 * rows + 8 : 2 * rows + 9]
-        carried.append(expanded[2 * rows : 2 * rows + 1])
+        carried[c] = expanded[2 * rows : 2 * rows + 1]
         for i in range(per):
             state_out[c * per + i] = local[:, i * SUB : (i + 1) * SUB]
 
+        if c < chunks - 1:
+            first_send(c)
+
+    def first_send(c):
         @pl.when(here == 0)
         def _():
             for i in range(per):
                 state_copy(c * per + i).start()
+
+    extra_copy = remote(
+        state_out.at[pl.ds((chunks - 1) * per, per)], extra, extra_sem.at[0], extra_sem.at[1]
+    )
+
+    def early_send():
+        @pl.when(here == 1)
+        def _():
+            extra_copy.start()
+
+    def early_pass():
+        c = chunks - 1
+        g = c * CHUNK // group_width
+
+        @pl.when(here == 2)
+        def _():
+            extra_copy.wait_recv()
+            for i in range(per):
+                at = c * per + i
+                state_out[at] = (
+                    ready[at] + dot(c_ahead[g], extra[i]) * carried[c][:, i * SUB : (i + 1) * SUB]
+                ).astype(BF16)
+                state_copy(at).start()
+
+    def late_pass():
+        c = chunks - 1
+        g = c * CHUNK // group_width
+
+        @pl.when(here == 1)
+        def _():
+            extra_copy.wait_send()
+            for i in range(per):
+                at = c * per + i
+                state_copy(at).wait_recv()
+                state_out[at] = (
+                    dot(c_ahead[g], state_in[at]) * carried[c][:, i * SUB : (i + 1) * SUB]
+                ).astype(BF16)
+                state_copy(at).start()
+
+    def make_ready(cs):
+        @pl.when(middle)
+        def _():
+            for c in cs:
+                g = c * CHUNK // group_width
+                for i in range(per):
+                    at = c * per + i
+                    sent = dot(c_next[g], state_out[at])
+                    if at < 2 * kv_local:
+                        col = at % kv_local * ADIM
+                        sent = jnp.where(
+                            spare, kv[at // kv_local, :, col : col + ADIM].astype(F32), sent
+                        )
+                    ready[at] = sent
 
     def pass_on(c):
         g = c * CHUNK // group_width
@@ -699,20 +772,14 @@
             for i in range(per):
                 at = c * per + i
                 state_copy(at).wait_recv()
-                state = state_out[at].astype(F32) + state_in[at].astype(F32) * carried[c][
-                    :, i * SUB : (i + 1) * SUB
-                ]
-                sent = dot(c_next[g], state.astype(BF16))
-                if at < 2 * kv_local:
-                    col = at % kv_local * ADIM
-                    sent = jnp.where(
-                        spare, kv[at // kv_local, :, col : col + ADIM].astype(F32), sent
-                    )
-                state_out[at] = sent.astype(BF16)
+                state_out[at] = (
+                    ready[at]
+                    + dot(c_ahead[g], state_in[at]) * carried[c][:, i * SUB : (i + 1) * SUB]
+                ).astype(BF16)
                 state_copy(at).start()
 
     def arrive(c):
-        @pl.when(here == n - 1)
+        @pl.when(here >= (2 if c == chunks - 1 else n - 1))
         def _():
             for i in range(per):
                 state_copy(c * per + i).wait_recv()
@@ -764,21 +831,32 @@
             ]
         gate_entry[:, at : at + CHUNK] = gate_entry[:, at : at + CHUNK] * gate
 
+    squares = {}
+
     def finish(c):
         at = c * CHUNK
         g = at // group_width
         came = jnp.concatenate([state_in[c * per + i] for i in range(per)], axis=1)
-        gated[:, at : at + CHUNK] = (
-            gated[:, at : at + CHUNK]
-            + dot(c_groups[g], came) * gate_entry[:, at : at + CHUNK]
-        )
-        if (at + CHUNK) % group_width == 0:
-            left = at + CHUNK - group_width
-            value = gated[:, left : left + group_width]
-            mean = jnp.sum(value * value, axis=1, keepdims=True) * (1.0 / group_width)
-            mamba_ref[:, left : left + group_width] = (
-                value * lax.rsqrt(mean + EPSILON) * gain_ref[:, left : left + group_width]
-            ).astype(BF16)
+        if c == chunks - 1:
+            local = jnp.concatenate([extra[i] for i in range(per)], axis=1)
+            theirs = jnp.where(here == 2, unit, c_groups[g].astype(F32)).astype(BF16)
+            product = dot(theirs, came) + dot(c_own[g], local)
+        else:
+            product = dot(c_groups[g], came)
+        value = gated[:, at : at + CHUNK] + product * gate_entry[:, at : at + CHUNK]
+        gated[:, at : at + CHUNK] = value
+        for i in range(CHUNK // 128):
+            piece = value[:, i * 128 : (i + 1) * 128]
+            squares[g] = squares[g] + piece * piece if g in squares else piece * piece
+
+    def normalize(g):
+        left = g * group_width
+        mean = jnp.sum(squares[g], axis=1, keepdims=True) * (1.0 / group_width)
+        mamba_ref[:, left : left + group_width] = (
+            gated[:, left : left + group_width]
+            * lax.rsqrt(mean + EPSILON)
+            * gain_ref[:, left : left + group_width]
+        ).astype(BF16)
 
     fetches[11].wait()
 
@@ -793,7 +871,9 @@
         def _():
             c_back.wait_recv()
             for g in range(groups):
-                c_next[g] = jnp.where(ahead, c_next[g].astype(F32), unit).astype(BF16)
+                theirs = c_next[g].astype(F32)
+                c_ahead[g] = jnp.where(ahead, theirs, 0.0).astype(BF16)
+                c_next[g] = jnp.where(ahead, theirs, unit).astype(BF16)
 
     def take_rest():
         for fetch in fetches[12:]:
@@ -807,7 +887,9 @@
         attend(head, held[0])
 
     steps = {
-        "l": make_local, "p": pass_on, "r": arrive, "i": inside, "a": attend_next, "f": finish,
+        "l": make_local, "q": lambda c: make_ready(range(2 * c, 2 * c + 2)), "p": pass_on, "n": normalize,
+        "e": lambda _: early_send(), "x": lambda _: early_pass(), "y": lambda _: late_pass(),
+        "o": lambda _: first_send(chunks - 1), "r": arrive, "i": inside, "a": attend_next, "f": finish,
         "k": lambda _: take_keys(), "t": lambda _: take_turned(), "w": lambda _: take_rest(),
     }
     for name, low_end, high_end in ORDER:
@@ -853,15 +935,17 @@
     reach = max(1, n // 2)
     vmem = pl.BlockSpec(memory_space=pltpu.VMEM)
     dma = pltpu.SemaphoreType.DMA
-    if reach == 2 and rows == STATE and keys.shape[1] == CHUNK and width == 8 * CHUNK and (
+    if n == 4 and rows == STATE and keys.shape[1] == CHUNK and width == 8 * CHUNK and (
         queries.shape[1] == 8 * ADIM
     ):
         subs = width // SUB
         state = pltpu.VMEM((subs, STATE, SUB), BF16)
         turned = pltpu.VMEM((bc_width // (2 * STATE), rows, STATE), BF16)
         body = functools.partial(packed_kernel, n)
-        buffers = [pltpu.VMEM((2,) + keys.shape, BF16), state, state, turned, turned]
-        sems = [dma((2,)), dma((2,)), dma((subs,)), dma((subs,)), dma((2,))]
+        ready = pltpu.VMEM((subs, rows, SUB), F32)
+        buffers = [pltpu.VMEM((2,) + keys.shape, BF16), state, state, turned, turned, turned, ready]
+        buffers.append(pltpu.VMEM((CHUNK // SUB, STATE, SUB), BF16))
+        sems = [dma((2,)), dma((2,)), dma((subs,)), dma((subs,)), dma((2,)), dma((2,))]
     else:
         state = pltpu.VMEM((chunks, STATE, CHUNK), BF16)
         body = functools.partial(relay_kernel, n, reach)

time: 25.2 us -> 24.1 us (0.956)
  Pallas kernels: 24.4 us -> 23.3 us
    pallas_call x1, Pallas kernels: 23.5 us -> 22.4 us  [shards(): pl.pallas_call(body, out_shape=(pltpu.VMEM((rows, width), BF16), pltpu.VM...]
where the time goes in v3:
time: 24.1 us; the launch traced here: 24 us
  Pallas kernels  23.3 us (97%)
  between operations  0.64 us (3%)
    pallas_call x1, Pallas kernels, shards(): pl.pallas_call(body, out_shape=(pltpu.VMEM((rows, width), BF16), pltpu.VM...  22.4 us
    pallas_call x1, Pallas kernels, shards(): pl.pallas_call(write_out, out_shape=(jax.ShapeDtypeStruct((rows, width),...  0.89 us

profile of v3, /device:TPU:26, one launch (start us, length us, event | category | flops | bytes accessed | tf_op | source)
XLA Modules:
  0.0 24.0 jit_solution(13332128440277953583)
XLA Ops:
  0.6 22.4 %shard_map.167 = (bf16[128,2048]{1,0:T(8,128)(2,1)S(1)}, bf16[128,1024]{1,0:T(8,128)(2,1)S(1)}) custom-call(bf16[128,2048]{1,0:T(8,128)(2,1)} %x_hbm.1, bf16[128,512]{1,0:T(8,128)(2,1)} %bc_hbm.1, bf16[128,2048]{1,0:T(8,128)(2,1)} %z_hbm.1, f32[32,128]{1,0:T(8,128)} %bitcast.7, f32[4,2048]{1,0:T(4,128)} %cxw_hbm.1, f32[1,2048]{1,0:T(1,128)} %bitcast.8, ...), custom_call_target="tpu_custom_call" | custom-call | tf_op jit(solution)/shard_map/pallas_call | solution.py:954
  23.1 0.9 %shard_map.168 = (bf16[128,2048]{1,0:T(8,128)(2,1)}, bf16[128,1024]{1,0:T(8,128)(2,1)}) custom-call(bf16[128,2048]{1,0:T(8,128)(2,1)S(1)} %get-tuple-element.4.mamba_ref, bf16[128,1024]{1,0:T(8,128)(2,1)S(1)} %get-tuple-element.5.attn_ref), custom_call_target="tpu_custom_call" | custom-call | tf_op jit(solution)/shard_map/pallas_call | solution.py:982

commit v4 on v3

--- a/solution.py
+++ b/solution.py
@@ -403,15 +403,18 @@
 
 
 SUB = 128
+EARLY = 2
 ORDER = (
+    ("l", 6, 7),
+    ("e", 6, 7),
     ("l", 7, 8),
-    ("e", 0, 1),
-    ("l", 0, 7),
-    ("o", 0, 1),
+    ("e", 7, 8),
+    ("l", 0, 6),
+    ("o", 6, 8),
     ("k", 0, 1),
     ("t", 0, 1),
     ("q", 0, 4),
-    ("x", 0, 1),
+    ("x", 6, 8),
     ("p", 0, 1),
     ("w", 0, 1),
     ("i", 0, 4),
@@ -424,22 +427,22 @@
     ("a", 3, 6),
     ("p", 4, 5),
     ("a", 6, 8),
-    ("p", 5, 7),
+    ("p", 5, 6),
     ("f", 0, 2),
     ("r", 2, 3),
     ("f", 2, 3),
     ("r", 3, 4),
     ("f", 3, 4),
     ("n", 0, 1),
-    ("y", 0, 1),
+    ("y", 6, 8),
     ("r", 4, 5),
     ("f", 4, 5),
+    ("r", 6, 7),
+    ("f", 6, 7),
+    ("r", 7, 8),
+    ("f", 7, 8),
     ("r", 5, 6),
     ("f", 5, 6),
-    ("r", 7, 8),
-    ("f", 7, 8),
-    ("r", 6, 7),
-    ("f", 6, 7),
     ("n", 1, 2),
 )
 
@@ -702,7 +705,7 @@
         for i in range(per):
             state_out[c * per + i] = local[:, i * SUB : (i + 1) * SUB]
 
-        if c < chunks - 1:
+        if c < chunks - EARLY:
             first_send(c)
 
     def first_send(c):
@@ -711,42 +714,45 @@
             for i in range(per):
                 state_copy(c * per + i).start()
 
-    extra_copy = remote(
-        state_out.at[pl.ds((chunks - 1) * per, per)], extra, extra_sem.at[0], extra_sem.at[1]
-    )
-
-    def early_send():
+    def extra_copy(c):
+        i = c - (chunks - EARLY)
+        return remote(
+            state_out.at[pl.ds(c * per, per)],
+            extra.at[pl.ds(i * per, per)],
+            extra_sem.at[0, i],
+            extra_sem.at[1, i],
+        )
+
+    def early_send(c):
         @pl.when(here == 1)
         def _():
-            extra_copy.start()
-
-    def early_pass():
-        c = chunks - 1
+            extra_copy(c).start()
+
+    def share(c, i):
+        return carried[c][:, i * SUB : (i + 1) * SUB]
+
+    def early_pass(c):
         g = c * CHUNK // group_width
 
         @pl.when(here == 2)
         def _():
-            extra_copy.wait_recv()
+            extra_copy(c).wait_recv()
             for i in range(per):
                 at = c * per + i
-                state_out[at] = (
-                    ready[at] + dot(c_ahead[g], extra[i]) * carried[c][:, i * SUB : (i + 1) * SUB]
-                ).astype(BF16)
+                early = extra[at - (chunks - EARLY) * per]
+                state_out[at] = (ready[at] + dot(c_ahead[g], early) * share(c, i)).astype(BF16)
                 state_copy(at).start()
 
-    def late_pass():
-        c = chunks - 1
+    def late_pass(c):
         g = c * CHUNK // group_width
 
         @pl.when(here == 1)
         def _():
-            extra_copy.wait_send()
+            extra_copy(c).wait_send()
             for i in range(per):
                 at = c * per + i
                 state_copy(at).wait_recv()
-                state_out[at] = (
-                    dot(c_ahead[g], state_in[at]) * carried[c][:, i * SUB : (i + 1) * SUB]
-                ).astype(BF16)
+                state_out[at] = (dot(c_ahead[g], state_in[at]) * share(c, i)).astype(BF16)
                 state_copy(at).start()
 
     def make_ready(cs):
@@ -779,13 +785,12 @@
                 state_copy(at).start()
 
     def arrive(c):
-        @pl.when(here >= (2 if c == chunks - 1 else n - 1))
+        @pl.when(here >= (2 if c >= chunks - EARLY else n - 1))
         def _():
             for i in range(per):
                 state_copy(c * per + i).wait_recv()
 
-    share = q_ref.shape[1] // (ADIM * kv_local)
-    q_heads = kv_local * share
+    per_kv = q_ref.shape[1] // (ADIM * kv_local)
     scale = ADIM**-0.5 * LOG2E
 
     def permitted_keys():
@@ -794,7 +799,7 @@
         return (doc_of(key_pos) == wide(doc_i, count)) & (key_pos <= wide(pos_i, count))
 
     def attend(head, permitted):
-        g = head // share
+        g = head // per_kv
         cols = slice(g * ADIM, (g + 1) * ADIM)
         keys = jnp.concatenate([state_in[g], kv[0, :, cols], k_ref[:, cols]], axis=0)
         values = jnp.concatenate([state_in[kv_local + g], kv[1, :, cols], v_ref[:, cols]], axis=0)
@@ -837,8 +842,9 @@
         at = c * CHUNK
         g = at // group_width
         came = jnp.concatenate([state_in[c * per + i] for i in range(per)], axis=1)
-        if c == chunks - 1:
-            local = jnp.concatenate([extra[i] for i in range(per)], axis=1)
+        if c >= chunks - EARLY:
+            base = (c - (chunks - EARLY)) * per
+            local = jnp.concatenate([extra[base + i] for i in range(per)], axis=1)
             theirs = jnp.where(here == 2, unit, c_groups[g].astype(F32)).astype(BF16)
             product = dot(theirs, came) + dot(c_own[g], local)
         else:
@@ -888,8 +894,7 @@
 
     steps = {
         "l": make_local, "q": lambda c: make_ready(range(2 * c, 2 * c + 2)), "p": pass_on, "n": normalize,
-        "e": lambda _: early_send(), "x": lambda _: early_pass(), "y": lambda _: late_pass(),
-        "o": lambda _: first_send(chunks - 1), "r": arrive, "i": inside, "a": attend_next, "f": finish,
+        "e": early_send, "x": early_pass, "y": late_pass, "o": first_send, "r": arrive, "i": inside, "a": attend_next, "f": finish,
         "k": lambda _: take_keys(), "t": lambda _: take_turned(), "w": lambda _: take_rest(),
     }
     for name, low_end, high_end in ORDER:
@@ -944,8 +949,8 @@
         body = functools.partial(packed_kernel, n)
         ready = pltpu.VMEM((subs, rows, SUB), F32)
         buffers = [pltpu.VMEM((2,) + keys.shape, BF16), state, state, turned, turned, turned, ready]
-        buffers.append(pltpu.VMEM((CHUNK // SUB, STATE, SUB), BF16))
-        sems = [dma((2,)), dma((2,)), dma((subs,)), dma((subs,)), dma((2,)), dma((2,))]
+        buffers.append(pltpu.VMEM((EARLY * CHUNK // SUB, STATE, SUB), BF16))
+        sems = [dma((2,)), dma((2,)), dma((subs,)), dma((subs,)), dma((2,)), dma((2, EARLY))]
     else:
         state = pltpu.VMEM((chunks, STATE, CHUNK), BF16)
         body = functools.partial(relay_kernel, n, reach)

time: 24.1 us -> 23.4 us (0.971)
  Pallas kernels: 23.3 us -> 22.6 us
    pallas_call x1, Pallas kernels: 22.4 us -> 21.7 us  [shards(): pl.pallas_call(body, out_shape=(pltpu.VMEM((rows, width), BF16), pltpu.VM...]
where the time goes in v4:
time: 23.4 us; the launch traced here: 23.3 us
  Pallas kernels  22.6 us (97%)
  between operations  0.64 us (3%)
    pallas_call x1, Pallas kernels, shards(): pl.pallas_call(body, out_shape=(pltpu.VMEM((rows, width), BF16), pltpu.VM...  21.7 us
    pallas_call x1, Pallas kernels, shards(): pl.pallas_call(write_out, out_shape=(jax.ShapeDtypeStruct((rows, width),...  0.89 us

profile of v4, /device:TPU:26, one launch (start us, length us, event | category | flops | bytes accessed | tf_op | source)
XLA Modules:
  0.0 23.3 jit_solution(10984442648779741973)
XLA Ops:
  0.6 21.7 %shard_map.167 = (bf16[128,2048]{1,0:T(8,128)(2,1)S(1)}, bf16[128,1024]{1,0:T(8,128)(2,1)S(1)}) custom-call(bf16[128,2048]{1,0:T(8,128)(2,1)} %x_hbm.1, bf16[128,512]{1,0:T(8,128)(2,1)} %bc_hbm.1, bf16[128,2048]{1,0:T(8,128)(2,1)} %z_hbm.1, f32[32,128]{1,0:T(8,128)} %bitcast.7, f32[4,2048]{1,0:T(4,128)} %cxw_hbm.1, f32[1,2048]{1,0:T(1,128)} %bitcast.8, ...), custom_call_target="tpu_custom_call" | custom-call | tf_op jit(solution)/shard_map/pallas_call | solution.py:959
  22.4 0.9 %shard_map.168 = (bf16[128,2048]{1,0:T(8,128)(2,1)}, bf16[128,1024]{1,0:T(8,128)(2,1)}) custom-call(bf16[128,2048]{1,0:T(8,128)(2,1)S(1)} %get-tuple-element.4.mamba_ref, bf16[128,1024]{1,0:T(8,128)(2,1)S(1)} %get-tuple-element.5.attn_ref), custom_call_target="tpu_custom_call" | custom-call | tf_op jit(solution)/shard_map/pallas_call | solution.py:987

commit v5 on v4

--- a/solution.py
+++ b/solution.py
@@ -410,6 +410,7 @@
     ("l", 7, 8),
     ("e", 7, 8),
     ("l", 0, 6),
+    ("u", 0, 1),
     ("o", 6, 8),
     ("k", 0, 1),
     ("t", 0, 1),
@@ -421,23 +422,27 @@
     ("p", 1, 2),
     ("i", 4, 8),
     ("p", 2, 3),
-    ("r", 0, 2),
+    ("r", 0, 1),
     ("a", 0, 3),
     ("p", 3, 4),
     ("a", 3, 6),
     ("p", 4, 5),
     ("a", 6, 8),
     ("p", 5, 6),
-    ("f", 0, 2),
+    ("y", 6, 7),
+    ("f", 0, 1),
+    ("r", 1, 2),
+    ("f", 1, 2),
     ("r", 2, 3),
     ("f", 2, 3),
     ("r", 3, 4),
     ("f", 3, 4),
     ("n", 0, 1),
-    ("y", 6, 8),
+    ("y", 7, 8),
     ("r", 4, 5),
     ("f", 4, 5),
     ("r", 6, 7),
+    ("g", 0, 8),
     ("f", 6, 7),
     ("r", 7, 8),
     ("f", 7, 8),
@@ -463,6 +468,7 @@
     c_ahead,
     ready,
     extra,
+    weights,
     xf,
     bcf,
     xc,
@@ -571,6 +577,9 @@
     def _():
         halo_copy.start()
         own_k.start()
+
+    @pl.when(middle)
+    def _():
         own_v.start()
 
     for fetch in fetches[2:11]:
@@ -688,6 +697,7 @@
     per_chunk = CHUNK // HDIM
     low_half = lax.broadcasted_iota(jnp.int32, (rows, 128), 1) < HDIM
     carried = {}
+    value_base = (chunks - EARLY) * per
 
     def make_local(c):
         at = c * CHUNK
@@ -748,26 +758,34 @@
 
         @pl.when(here == 1)
         def _():
+            if c == chunks - EARLY:
+                own_v.wait_recv()
             extra_copy(c).wait_send()
             for i in range(per):
                 at = c * per + i
                 state_copy(at).wait_recv()
-                state_out[at] = (dot(c_ahead[g], state_in[at]) * share(c, i)).astype(BF16)
+                sent = dot(c_ahead[g], state_in[at]) * share(c, i)
+                if value_base <= at < value_base + kv_local:
+                    col = (at - value_base) * ADIM
+                    sent = jnp.where(spare, kv[1, :, col : col + ADIM].astype(F32), sent)
+                state_out[at] = sent.astype(BF16)
                 state_copy(at).start()
 
     def make_ready(cs):
-        @pl.when(middle)
+        cs = list(cs)
+
+        @pl.when(middle if cs[-1] < chunks - EARLY else here == 2)
         def _():
             for c in cs:
                 g = c * CHUNK // group_width
                 for i in range(per):
                     at = c * per + i
                     sent = dot(c_next[g], state_out[at])
-                    if at < 2 * kv_local:
-                        col = at % kv_local * ADIM
-                        sent = jnp.where(
-                            spare, kv[at // kv_local, :, col : col + ADIM].astype(F32), sent
-                        )
+                    for base, slot in ((0, 0), (value_base, 1)):
+                        if base <= at < base + kv_local:
+                            col = (at - base) * ADIM
+                            far = kv[slot, :, col : col + ADIM].astype(F32)
+                            sent = jnp.where(spare, far, sent)
                     ready[at] = sent
 
     def pass_on(c):
@@ -798,19 +816,28 @@
         key_pos = first - 2 * rows + lax.broadcasted_iota(jnp.int32, (rows, count), 1)
         return (doc_of(key_pos) == wide(doc_i, count)) & (key_pos <= wide(pos_i, count))
 
-    def attend(head, permitted):
+    totals = []
+
+    def weigh(head, permitted):
         g = head // per_kv
         cols = slice(g * ADIM, (g + 1) * ADIM)
         keys = jnp.concatenate([state_in[g], kv[0, :, cols], k_ref[:, cols]], axis=0)
-        values = jnp.concatenate([state_in[kv_local + g], kv[1, :, cols], v_ref[:, cols]], axis=0)
         query = q_ref[:, head * ADIM : (head + 1) * ADIM]
         scores = lax.dot_general(query, keys, NT, preferred_element_type=F32)
         scores = jnp.where(permitted, scores, NEGATIVE)
         peak = jnp.max(scores, axis=1, keepdims=True)
         expo = jnp.exp2((scores - peak) * scale)
-        total = jnp.sum(expo, axis=1, keepdims=True)
-        summed = dot(expo.astype(BF16), values)
-        attn_ref[:, head * ADIM : (head + 1) * ADIM] = (summed / total).astype(BF16)
+        totals.append(jnp.sum(expo, axis=1, keepdims=True))
+        weights[head] = expo.astype(BF16)
+
+    def gather(head):
+        g = head // per_kv
+        cols = slice(g * ADIM, (g + 1) * ADIM)
+        values = jnp.concatenate(
+            [state_in[value_base + g], kv[1, :, cols], v_ref[:, cols]], axis=0
+        )
+        summed = dot(weights[head], values)
+        attn_ref[:, head * ADIM : (head + 1) * ADIM] = (summed / totals[head]).astype(BF16)
 
     def inside(c):
         at = c * CHUNK
@@ -870,7 +897,15 @@
         @pl.when(has_left)
         def _():
             own_k.wait_recv()
+
+        @pl.when(here >= 2)
+        def _():
             own_v.wait_recv()
+
+    def send_values():
+        @pl.when(here == 0)
+        def _():
+            own_v.start()
 
     def take_turned():
         @pl.when(middle)
@@ -890,10 +925,11 @@
     def attend_next(head):
         if not held:
             held.append(permitted_keys())
-        attend(head, held[0])
+        weigh(head, held[0])
 
     steps = {
-        "l": make_local, "q": lambda c: make_ready(range(2 * c, 2 * c + 2)), "p": pass_on, "n": normalize,
+        "l": make_local, "q": lambda c: make_ready(range(2 * c, 2 * c + 2)), "g": gather,
+        "u": lambda _: send_values(), "p": pass_on, "n": normalize,
         "e": early_send, "x": early_pass, "y": late_pass, "o": first_send, "r": arrive, "i": inside, "a": attend_next, "f": finish,
         "k": lambda _: take_keys(), "t": lambda _: take_turned(), "w": lambda _: take_rest(),
     }
@@ -950,6 +986,7 @@
         ready = pltpu.VMEM((subs, rows, SUB), F32)
         buffers = [pltpu.VMEM((2,) + keys.shape, BF16), state, state, turned, turned, turned, ready]
         buffers.append(pltpu.VMEM((EARLY * CHUNK // SUB, STATE, SUB), BF16))
+        buffers.append(pltpu.VMEM((queries.shape[1] // ADIM, rows, 3 * rows), BF16))
         sems = [dma((2,)), dma((2,)), dma((subs,)), dma((subs,)), dma((2,)), dma((2, EARLY))]
     else:
         state = pltpu.VMEM((chunks, STATE, CHUNK), BF16)

time: 23.4 us -> 23 us (0.983)
  Pallas kernels: 22.6 us -> 22.2 us
    pallas_call x1, Pallas kernels: 21.7 us -> 21.3 us  [shards(): pl.pallas_call(body, out_shape=(pltpu.VMEM((rows, width), BF16), pltpu.VM...]
where the time goes in v5:
time: 23 us; the launch traced here: 22.9 us
  Pallas kernels  22.2 us (97%)
  between operations  0.64 us (3%)
    pallas_call x1, Pallas kernels, shards(): pl.pallas_call(body, out_shape=(pltpu.VMEM((rows, width), BF16), pltpu.VM...  21.3 us
    pallas_call x1, Pallas kernels, shards(): pl.pallas_call(write_out, out_shape=(jax.ShapeDtypeStruct((rows, width),...  0.89 us

profile of v5, /device:TPU:26, one launch (start us, length us, event | category | flops | bytes accessed | tf_op | source)
XLA Modules:
  0.0 22.9 jit_solution(3458582805144215521)
XLA Ops:
  0.6 21.3 %shard_map.167 = (bf16[128,2048]{1,0:T(8,128)(2,1)S(1)}, bf16[128,1024]{1,0:T(8,128)(2,1)S(1)}) custom-call(bf16[128,2048]{1,0:T(8,128)(2,1)} %x_hbm.1, bf16[128,512]{1,0:T(8,128)(2,1)} %bc_hbm.1, bf16[128,2048]{1,0:T(8,128)(2,1)} %z_hbm.1, f32[32,128]{1,0:T(8,128)} %bitcast.7, f32[4,2048]{1,0:T(4,128)} %cxw_hbm.1, f32[1,2048]{1,0:T(1,128)} %bitcast.8, ...), custom_call_target="tpu_custom_call" | custom-call | tf_op jit(solution)/shard_map/pallas_call | solution.py:996
  22.0 0.9 %shard_map.168 = (bf16[128,2048]{1,0:T(8,128)(2,1)}, bf16[128,1024]{1,0:T(8,128)(2,1)}) custom-call(bf16[128,2048]{1,0:T(8,128)(2,1)S(1)} %get-tuple-element.4.mamba_ref, bf16[128,1024]{1,0:T(8,128)(2,1)S(1)} %get-tuple-element.5.attn_ref), custom_call_target="tpu_custom_call" | custom-call | tf_op jit(solution)/shard_map/pallas_call | solution.py:1024

commit v6 on v5

--- a/solution.py
+++ b/solution.py
@@ -426,9 +426,8 @@
     ("a", 0, 3),
     ("p", 3, 4),
     ("a", 3, 6),
-    ("p", 4, 5),
+    ("p", 4, 6),
     ("a", 6, 8),
-    ("p", 5, 6),
     ("y", 6, 7),
     ("f", 0, 1),
     ("r", 1, 2),

time: 23 us -> 23 us (level)
  no operation moved by 1% of the time
where the time goes in v6:
time: 23 us; the launch traced here: 22.9 us
  Pallas kernels  22.2 us (97%)
  between operations  0.64 us (3%)
    pallas_call x1, Pallas kernels, shards(): pl.pallas_call(body, out_shape=(pltpu.VMEM((rows, width), BF16), pltpu.VM...  21.3 us
    pallas_call x1, Pallas kernels, shards(): pl.pallas_call(write_out, out_shape=(jax.ShapeDtypeStruct((rows, width),...  0.89 us

profile of v6, /device:TPU:26, one launch (start us, length us, event | category | flops | bytes accessed | tf_op | source)
XLA Modules:
  0.0 22.9 jit_solution(7679445997919560110)
XLA Ops:
  0.6 21.3 %shard_map.167 = (bf16[128,2048]{1,0:T(8,128)(2,1)S(1)}, bf16[128,1024]{1,0:T(8,128)(2,1)S(1)}) custom-call(bf16[128,2048]{1,0:T(8,128)(2,1)} %x_hbm.1, bf16[128,512]{1,0:T(8,128)(2,1)} %bc_hbm.1, bf16[128,2048]{1,0:T(8,128)(2,1)} %z_hbm.1, f32[32,128]{1,0:T(8,128)} %bitcast.7, f32[4,2048]{1,0:T(4,128)} %cxw_hbm.1, f32[1,2048]{1,0:T(1,128)} %bitcast.8, ...), custom_call_target="tpu_custom_call" | custom-call | tf_op jit(solution)/shard_map/pallas_call | solution.py:995
  22.0 0.9 %shard_map.168 = (bf16[128,2048]{1,0:T(8,128)(2,1)}, bf16[128,1024]{1,0:T(8,128)(2,1)}) custom-call(bf16[128,2048]{1,0:T(8,128)(2,1)S(1)} %get-tuple-element.4.mamba_ref, bf16[128,1024]{1,0:T(8,128)(2,1)S(1)} %get-tuple-element.5.attn_ref), custom_call_target="tpu_custom_call" | custom-call | tf_op jit(solution)/shard_map/pallas_call | solution.py:1023
